TPU v7x, 512 devices: a whole 4x8x8 slice. The times are simulated.
512 devices in a mesh: seq: 64 (over y, x, core), head: 8 (over z).
Axes of the slice: x: 4, y: 8, z: 8, core: 2. Of those that a mesh axis runs over, the one named last changes fastest.
Arguments:
- activations: bfloat16 [16384, 4096], P('seq', 'head'), may hold values from -6 to 6
- grad_out: bfloat16 [16384, 4096], P('seq', 'head'), may hold values from -0.03125 to 0.03125
- query_weight: bfloat16 [4096, 4096], P('seq', 'head'), may hold values from -0.09375 to 0.09375
- key_weight: bfloat16 [4096, 1024], P('seq', 'head'), may hold values from -0.09375 to 0.09375
- value_weight: bfloat16 [4096, 1024], P('seq', 'head'), may hold values from -0.09375 to 0.09375
Outputs:
- grad_input: bfloat16 [16384, 4096], P('seq', 'head')
All inputs are finite; a program needn't handle non-finite values.
Results may differ from a plain program's by a relative error of at most 0.018.
Values may be sent and summed in bfloat16 or wider, within the bound.
A program may use at most 64 MiB of HBM per device.

v0:
```python
import jax
import jax.numpy as jnp
from jax import lax
from jax.sharding import Mesh
from jax.sharding import PartitionSpec as P

HEADS = 32
KV_HEADS = 8
HEAD_DIM = 128
SEQ = ("seq_0", "seq_1", "seq_2")


def in_one_piece(arrays, axis, dim, along):
    both = jnp.concatenate(arrays, axis=along)
    out, at, done = (lax.all_gather(both, axis, axis=dim, tiled=True), 0, [])
    for a in arrays:
        done.append(lax.slice_in_dim(out, at, at + a.shape[along], axis=along))
        at += a.shape[along]
    return tuple(done)


def laid_out(blocks, dim):
    dims = list(blocks.shape[1:])
    dims[dim] *= blocks.shape[0]
    return jnp.moveaxis(blocks, 0, dim).reshape(dims)


def from_everyone(shard, axis):
    copies = jnp.broadcast_to(shard, (lax.axis_size(axis), *shard.shape))
    return lax.all_to_all(copies, axis, split_axis=0, concat_axis=0, tiled=True)


def gather_directly(shard, axis, dim):
    return laid_out(from_everyone(shard, axis), dim)


def nothing_yet(shard, identity):
    return jnp.zeros_like(shard) + jnp.asarray(identity, shard.dtype)


def entering(shard, axes, combine, identity, reverse):
    before = start = nothing_yet(shard, identity)
    so_far = shard
    for axis in reversed(axes):
        size, position = (lax.axis_size(axis), lax.axis_index(axis))
        pieces = lax.all_gather(so_far.astype(jnp.bfloat16), axis)
        inside, so_far = (start, start)
        for k in reversed(range(size)) if reverse else range(size):
            passed = k > position if reverse else k < position
            so_far = combine(so_far, pieces[k].astype(shard.dtype))
            inside = jnp.where(passed, so_far, inside)
        before = combine(inside, before)
    return before


def add_states(earlier, later):
    return earlier + later


def contract_rows(grads, weight):
    return lax.dot_general(
        grads, weight, (((1,), (1,)), ((), ())), preferred_element_type=jnp.float32
    )


def local(activations, grad_out, query_weight, key_weight, value_weight):
    factor = HEAD_DIM ** (-0.5)
    group_size = HEADS // KV_HEADS
    gathered = in_one_piece((query_weight, key_weight, value_weight), SEQ, 0, 1)
    query_full, key_full, value_full = gathered
    tokens_dev = activations.shape[0]
    portion = gather_directly(activations, "head", 1)
    projected = tuple(
        (jnp.dot(portion, weight, preferred_element_type=jnp.float32) for weight in gathered)
    )
    queries, key_rows, value_rows = tuple((item.astype(jnp.bfloat16) for item in projected))
    kv_groups = key_full.shape[1] // HEAD_DIM
    query_heads = queries.reshape(tokens_dev, kv_groups, group_size, HEAD_DIM)
    key_heads = key_rows.reshape(tokens_dev, kv_groups, HEAD_DIM)
    value_heads = value_rows.reshape(tokens_dev, kv_groups, HEAD_DIM)
    grad_heads = grad_out.reshape(tokens_dev, kv_groups, group_size, HEAD_DIM)
    kv_state = jnp.einsum(
        "tgd,tge->gde", key_heads, value_heads, preferred_element_type=jnp.float32
    ).astype(jnp.bfloat16)
    grad_state = (
        factor
        * jnp.einsum("tghd,tghe->gde", query_heads, grad_heads, preferred_element_type=jnp.float32)
    ).astype(jnp.bfloat16)
    kv_state, grad_state = lax.optimization_barrier((kv_state, grad_state))
    kv_wide = kv_state.astype(jnp.float32)
    grad_wide = grad_state.astype(jnp.float32)
    prefix = entering(kv_wide, SEQ, add_states, jnp.zeros_like(kv_wide), False)
    suffix = entering(grad_wide, SEQ, add_states, jnp.zeros_like(grad_wide), True)
    prefix_half = prefix.astype(jnp.bfloat16)
    suffix_half = suffix.astype(jnp.bfloat16)
    causal = jnp.arange(tokens_dev)[:, None] >= jnp.arange(tokens_dev)[None, :]
    scores = jnp.where(
        causal,
        jnp.einsum("tghd,sgd->ghts", query_heads, key_heads, preferred_element_type=jnp.float32),
        0.0,
    ).astype(jnp.bfloat16)
    grad_scores = jnp.where(
        causal,
        jnp.einsum("tghe,sge->ghts", grad_heads, value_heads, preferred_element_type=jnp.float32),
        0.0,
    ).astype(jnp.bfloat16)
    grad_query = factor * (
        jnp.einsum("ghts,sgd->tghd", grad_scores, key_heads, preferred_element_type=jnp.float32)
        + jnp.einsum("tghe,gde->tghd", grad_heads, prefix_half, preferred_element_type=jnp.float32)
    )
    grad_key = factor * jnp.einsum(
        "ghts,tghd->sgd", grad_scores, query_heads, preferred_element_type=jnp.float32
    ) + jnp.einsum("sge,gde->sgd", value_heads, suffix_half, preferred_element_type=jnp.float32)
    grad_value = factor * jnp.einsum(
        "ghts,tghe->sge", scores, grad_heads, preferred_element_type=jnp.float32
    ) + jnp.einsum("sgd,gde->sge", key_heads, suffix_half, preferred_element_type=jnp.float32)
    grad_query = grad_query.astype(jnp.bfloat16).reshape(tokens_dev, -1)
    grad_key = grad_key.astype(jnp.bfloat16).reshape(tokens_dev, -1)
    grad_value = grad_value.astype(jnp.bfloat16).reshape(tokens_dev, -1)
    partial_input = (
        contract_rows(grad_query, query_full)
        + contract_rows(grad_key, key_full)
        + contract_rows(grad_value, value_full)
    )
    return lax.psum_scatter(
        partial_input.astype(jnp.bfloat16), "head", scatter_dimension=1, tiled=True
    )


def solution(mesh):
    finer = Mesh(
        mesh.devices.reshape(8, 4, 2, mesh.shape["head"]), ("seq_0", "seq_1", "seq_2", "head")
    )
    return jax.shard_map(
        local,
        mesh=finer,
        in_specs=(P(SEQ, "head"), P(SEQ, "head"), P(SEQ, "head"), P(SEQ, "head"), P(SEQ, "head")),
        out_specs=P(SEQ, "head"),
        check_vma=False,
    )
```

profile of v0, /device:TPU:1, one launch (start us, length us, event | category | flops | bytes accessed | tf_op | source)
XLA Modules:
  0.0 250.6 jit_solution(18276633968155749317)
XLA Ops:
  6.5 0.0 copy-start
  6.5 0.0 all-gather.4.cloned.1.call-start
  6.5 1.6 pad_maximum_fusion
  8.1 0.0 all-gather.4.cloned.1.call-update
  8.1 1.1 copy.27
  9.2 1.5 broadcast_in_dim.17
  10.7 10.9 %all-to-all-start = ((bf16[8,256,512]{1,2,0:T(8,128)(2,1)}), bf16[8,256,512]{1,2,0:T(8,128)(2,1)S(1)}, u32[]{:S(2)}, u32[]{:S(2)}) async-start(bf16[8,256,512]{1,2,0:T(8,128)(2,1)} %broadcast_in_dim.17), calls=%async_computation | async-start | bytes 4194304 | tf_op jit(solution)/shard_map/all_to_all | solution.py:30
  21.6 0.0 reduce-scatter.2.cloned.1.call-start
  21.7 48.3 %all-to-all-done = bf16[8,256,512]{1,2,0:T(8,128)(2,1)S(1)} async-done(((bf16[8,256,512]{1,2,0:T(8,128)(2,1)}), bf16[8,256,512]{1,2,0:T(8,128)(2,1)S(1)}, u32[]{:S(2)}, u32[]{:S(2)}) %all-to-all-start) | async-done | bytes 2097184 | tf_op jit(solution)/shard_map/all_to_all | solution.py:30
  70.0 33.0 %all-gather.4.cloned.1.call-done = bf16[4096,768]{1,0:T(8,128)(2,1)} async-done(((bf16[64,768]{1,0:T(8,128)(2,1)}), bf16[4096,768]{1,0:T(8,128)(2,1)}) %all-gather.4.cloned.1.call-update) | async-done | bytes 6291472 | tf_op jit(solution)/shard_map/all_gather | solution.py:15
  103.0 3.5 %fusion.13 = bf16[512,256]{1,0:T(8,128)(2,1)S(1)} fusion(bf16[256,4096]{0,1:T(8,128)(2,1)S(1)} %bitcast.181, bf16[4096,768]{1,0:T(8,128)(2,1)} %all-gather.4.cloned.1.call-done), kind=kOutput, calls=%fused_computation.19 | convolution fusion | flops 1073872896 | bytes 6553600 | tf_op jit(solution)/shard_map/dot_general | solution.py:74
  106.5 0.0 copy-done
  106.5 0.2 fusion.29
  106.7 1.8 convolution_convert_fusion.1
  108.5 1.8 convolution_convert_fusion
  110.3 0.2 fusion.28
  110.5 1.9 all-gather.1
  112.3 9.1 %all_gather.38 = bf16[4,1,128,128]{3,2,1,0:T(8,128)(2,1)S(1)} all-gather(bf16[1,1,128,128]{3,2,1,0:T(8,128)(2,1)S(1)} %fusion.84), channel_id=1, replica_groups=mesh['seq_0'=8,'seq_1'=4,'seq_2'=2,'head'=8] {'seq_1'}, dimensions={0}, use_global_device_ids=true | all-gather | bytes 163840 | tf_op jit(solution)/shard_map/all_gather | solution.py:46
  121.5 18.8 %all_gather.39 = bf16[8,1,128,128]{3,2,1,0:T(8,128)(2,1)S(1)} all-gather(bf16[1,1,128,128]{3,2,1,0:T(8,128)(2,1)S(1)} %fusion.80), channel_id=1, replica_groups=mesh['seq_0'=8,'seq_1'=4,'seq_2'=2,'head'=8] {'seq_0'}, dimensions={0}, use_global_device_ids=true | all-gather | bytes 294912 | tf_op jit(solution)/shard_map/all_gather | solution.py:46
  140.3 0.1 fusion.62
  140.4 0.2 fusion.86
  140.6 0.1 fusion.88
  140.8 0.3 fusion.9
  141.1 0.3 fusion.8
  141.4 10.9 %all-gather = bf16[2,128,128]{2,1,0:T(8,128)(2,1)S(1)} all-gather(bf16[1,128,128]{2,1,0:T(8,128)(2,1)S(1)} %fusion.28), channel_id=2, replica_groups=mesh['seq_0'=8,'seq_1'=4,'seq_2'=2,'head'=8] {'seq_2'}, dimensions={0}, use_global_device_ids=true | all-gather | bytes 98304 | tf_op jit(solution)/shard_map/all_gather | solution.py:46
  152.3 9.1 %all_gather.34 = bf16[4,1,128,128]{3,2,1,0:T(8,128)(2,1)S(1)} all-gather(bf16[1,1,128,128]{3,2,1,0:T(8,128)(2,1)S(1)} %fusion.83), channel_id=1, replica_groups=mesh['seq_0'=8,'seq_1'=4,'seq_2'=2,'head'=8] {'seq_1'}, dimensions={0}, use_global_device_ids=true | all-gather | bytes 163840 | tf_op jit(solution)/shard_map/all_gather | solution.py:46
  161.4 18.8 %all_gather.35 = bf16[8,1,128,128]{3,2,1,0:T(8,128)(2,1)S(1)} all-gather(bf16[1,1,128,128]{3,2,1,0:T(8,128)(2,1)S(1)} %fusion.82), channel_id=1, replica_groups=mesh['seq_0'=8,'seq_1'=4,'seq_2'=2,'head'=8] {'seq_0'}, dimensions={0}, use_global_device_ids=true | all-gather | bytes 294912 | tf_op jit(solution)/shard_map/all_gather | solution.py:46
  180.2 0.2 convolution_bitcast_fusion.3
  180.5 0.3 fusion.12
  180.7 4.5 %fusion.24 = f32[256,4096]{1,0:T(8,128)} fusion(f32[128,256]{1,0:T(8,128)S(1)} %fusion.88, bf16[256,4,128]{0,2,1:T(8,128)(2,1)S(1)} %bitcast.186, bf16[4,256,256]{1,2,0:T(8,128)(2,1)S(1)} %fusion.9, bf16[4096,768]{1,0:T(8,128)(2,1)} %all-gather.4.cloned.1.call-done), kind=kOutput, calls=%fused_computation.32 | convolution fusion | flops 335642624 | bytes 6160384 | tf_op jit(solution)/shard_map/dot_general | solution.py:61
  185.3 6.8 %convolution_add_fusion = f32[256,4096]{1,0:T(8,128)} fusion(f32[256,4096]{1,0:T(8,128)} %fusion.24, bf16[256,512]{0,1:T(8,128)(2,1)S(1)} %bitcast.187, bf16[4096,768]{1,0:T(8,128)(2,1)} %all-gather.4.cloned.1.call-done), kind=kOutput, calls=%fused_computation | convolution fusion | flops 1074790400 | bytes 12845056 | tf_op jit(solution)/shard_map/dot_general | solution.py:61
  192.1 4.8 %fusion = bf16[256,4096]{1,0:T(8,128)(2,1)} fusion(f32[256,4096]{1,0:T(8,128)} %convolution_add_fusion, f32[128,256]{0,1:T(8,128)S(1)} %fusion.86, bf16[4,256,256]{1,2,0:T(8,128)(2,1)S(1)} %fusion.8, bf16[4096,768]{1,0:T(8,128)(2,1)} %all-gather.4.cloned.1.call-done, bf16[256,512]{1,0:T(8,128)(2,1)S(1)} %copy-done), kind=kOutput, calls=%fused_computation.2 | convolution fusion | flops 337739776 | bytes 8257536 | tf_op jit(solution)/shard_map/dot_general | solution.py:61
  196.8 0.0 reduce-scatter.2.cloned.1.call-update
  196.9 46.9 %reduce-scatter.2.cloned.1.call-done = bf16[256,512]{1,0:T(8,128)(2,1)} async-done(((bf16[256,4096]{1,0:T(8,128)(2,1)}), bf16[256,512]{1,0:T(8,128)(2,1)}) %reduce-scatter.2.cloned.1.call-update) | async-done | bytes 262160 | tf_op jit(solution)/shard_map/reduce_scatter | solution.py:125
  (5 shorter events, 0.1 us)
Async XLA Ops:
  6.5 99.9 %copy-start = (bf16[256,512]{1,0:T(8,128)(2,1)S(1)}, bf16[256,512]{1,0:T(8,128)(2,1)}, u32[]{:S(2)}) copy-start(bf16[256,512]{1,0:T(8,128)(2,1)} %param.6) | copy-start | bytes 786436
  6.5 96.4 %all-gather.4.cloned.1.call-start = ((), (), s32[]{:S(2)}) async-start(), calls=%async_computation.2 | async-start | bytes 6389760 | tf_op jit(solution)/shard_map/all_gather | solution.py:15
  10.7 59.3 %all-to-all-start = ((bf16[8,256,512]{1,2,0:T(8,128)(2,1)}), bf16[8,256,512]{1,2,0:T(8,128)(2,1)S(1)}, u32[]{:S(2)}, u32[]{:S(2)}) async-start(bf16[8,256,512]{1,2,0:T(8,128)(2,1)} %broadcast_in_dim.17), calls=%async_computation | async-start | bytes 4194304 | tf_op jit(solution)/shard_map/all_to_all | solution.py:30
  21.6 222.2 %reduce-scatter.2.cloned.1.call-start = ((), (), s32[]{:S(2)}) async-start(), calls=%async_computation.3 | async-start | bytes 2359296 | tf_op jit(solution)/shard_map/reduce_scatter | solution.py:125
Sparse Core Ops, SparseCore 0:
  10.7 92.2 all-gather.3
  197.0 46.7 reduce-scatter.1
where the time goes:
time: 255 us; the launch traced here: 251 us
  waiting for transfers between devices  128 us (50%)
  blocking collectives  68.5 us (27%)
  matrix products  25 us (10%)
  between operations  13.6 us (5%)
  starting transfers between devices  10.9 us (4%)
  local copies, waits for them, and re-layouts  2.57 us (1%)
    all_gather x6, blocking collectives, entering(): pieces = lax.all_gather(so_far.astype(jnp.bfloat16), axis)  68.5 us
    all_to_all x1, waiting for transfers between devices, from_everyone(): return lax.all_to_all(copies, axis, split_axis=0, concat_axis=0, tiled=True)  48.3 us
    reduce_scatter x1, waiting for transfers between devices, local(): lax.psum_scatter(partial_input.astype(jnp.bfloat16), 'head', scatter_dime...  46.9 us
    all_gather x1, waiting for transfers between devices, in_one_piece(): out, at, done = (lax.all_gather(both, axis, axis=dim, tiled=True), 0, [])  33 us
    dot_general x3, matrix products, contract_rows(): lax.dot_general(grads, weight, (((1,), (1,)), ((), ())), preferred_elemen...  16.1 us
    all_to_all x1, starting transfers between devices, from_everyone(): return lax.all_to_all(copies, axis, split_axis=0, concat_axis=0, tiled=True)  10.9 us
    dot_general x3, matrix products, local(): jnp.dot(portion, weight, preferred_element_type=jnp.float32)  7.08 us
  transfers between devices with their start and end apart: 3, of which 3 were waited for; matrix products, arithmetic and copies ran while one was open for 1% of the time, Pallas kernels for 0%

commit v1 on v0

v1 whole, which is shorter than its diff:
```python
import jax
import jax.numpy as jnp
from jax import lax
from jax.experimental import pallas as pl
from jax.experimental.pallas import tpu as pltpu
from jax.sharding import Mesh
from jax.sharding import PartitionSpec as P

HEADS = 32
KV_HEADS = 8
HD = 128
GROUP = HEADS // KV_HEADS
NY, NX, NC, NZ = 8, 4, 2, 8
ROW = NX * NC
AXES = ("y", "x", "core", "head")
SEQ = ("y", "x", "core")
F32 = jnp.float32
BF16 = jnp.bfloat16
TOK = 256
FEAT = 512
WROWS = 64
WCOLS = 768
SUBS = 4
SUB = TOK // SUBS
HALF = NZ // 2
R_ORDER = (0, 1, 2, 3)
L_ORDER = (2, 3, 0, 1)
R_LAST = (0, 1)
L_LAST = (2, 3)
X_ORDER = (0, 1, 3, 2)
XR_LAST = (0, 1)
XL_LAST = (3, 2)


def nt(a, b):
    return lax.dot_general(a, b, (((1,), (1,)), ((), ())), preferred_element_type=F32)


def tn(a, b):
    return lax.dot_general(a, b, (((0,), (0,)), ((), ())), preferred_element_type=F32)


def nn(a, b):
    return jnp.dot(a, b, preferred_element_type=F32)


def kernel(
    a_ref, g_ref, wq_ref, wk_ref, wv_ref, o_ref,
    act, wts, acc, qkv, dq, dk, dv, grads, part, tx, rx,
    st, in1, tot, in2, out3, in3,
    z_send, z_recv, w_send, w_recv, s_send, s_recv, e_send, e_recv, r_send, r_recv,
):
    y, x, c, z = (lax.axis_index(n) for n in AXES)
    r = x * NC + c
    n_y = lambda d: lax.rem(y + d + NY, NY)
    n_x = lambda d: lax.rem(x + d + NX, NX)
    n_z = lambda d: lax.rem(z + d + NZ, NZ)
    n_r = lambda d: lax.rem(r + d + ROW, ROW)
    zr, zl = {"head": n_z(1)}, {"head": n_z(-1)}
    yr, yl = {"y": n_y(1)}, {"y": n_y(-1)}
    xr, xl = {"x": n_x(1)}, {"x": n_x(-1)}
    sib = {"core": 1 - c}
    row_peer = lambda d: {"x": n_r(d) // NC, "core": lax.rem(n_r(d), NC)}

    barrier = pltpu.get_barrier_semaphore()
    peers = [zr, zl] + [row_peer(d) for d in range(1, ROW)] + [{"y": n_y(d)} for d in range(1, NY)]
    for peer in peers:
        pl.semaphore_signal(barrier, inc=1, device_id=peer, device_id_type=pl.DeviceIdType.MESH)

    act[z] = a_ref[...]
    wts[y, x, c, :, 0:512] = wq_ref[...]
    wts[y, x, c, :, 512:640] = wk_ref[...]
    wts[y, x, c, :, 640:768] = wv_ref[...]
    pl.semaphore_wait(barrier, len(peers))

    def copy(src, dst, ssem, rsem, dev):
        return pltpu.make_async_remote_copy(
            src_ref=src, dst_ref=dst, send_sem=ssem, recv_sem=rsem,
            device_id=dev, device_id_type=pl.DeviceIdType.MESH,
        )

    def same(ref, ssem, rsem, dev):
        return copy(ref, ref, ssem, rsem, dev)

    def z_msg(d, k, s):
        origin = n_z(1 - k) if d == 0 else n_z(k - 1)
        ref = act.at[origin, pl.ds(s * SUB, SUB)]
        return same(ref, z_send.at[d, k, s], z_recv.at[d, k, s], zr if d == 0 else zl)

    def z_wait(d, k, s):
        origin = n_z(-k) if d == 0 else n_z(k)
        ref = act.at[origin, pl.ds(s * SUB, SUB)]
        same(ref, z_send.at[d, k, s], z_recv.at[d, k, s], zr if d == 0 else zl).wait_recv()

    def z_has(d, k, s):
        return k < HALF or (k == HALF and s in (R_LAST if d == 0 else L_LAST))

    def z_start():
        for i in range(SUBS):
            z_msg(0, 1, R_ORDER[i]).start()
            z_msg(1, 1, L_ORDER[i]).start()

    z_ticks = []
    for k in range(1, HALF + 1):
        for i in range(SUBS):
            pair = [(0, k, R_ORDER[i]), (1, k, L_ORDER[i])]
            pair = [p for p in pair if z_has(*p)]
            if pair:
                z_ticks.append(pair)

    def z_tick(i):
        for d, k, s in z_ticks[i]:
            z_wait(d, k, s)
            if z_has(d, k + 1, s):
                z_msg(d, k + 1, s).start()

    def w_ref(dy, dx, core, half=None):
        ref = wts.at[n_y(dy), n_x(dx), core]
        return ref if half is None else ref.at[pl.ds(32 * half, 32)]

    def w_msg(ref, i, dev):
        return same(ref, w_send.at[i], w_recv.at[i], dev)

    def sib_msg(m, core):
        ref = wts.at[n_y(m), :, core]
        return same(ref, s_send.at[m % NY], s_recv.at[m % NY], sib)

    def core0():
        slot = lambda d, k, j: 4 + (d * 5 + k) * 4 + j

        def has(d, k, j):
            return k < 4 or (k == 4 and j in (XR_LAST if d == 0 else XL_LAST))

        def y_msg(d, k, j):
            dy = (1 - k) if d == 0 else (k - 1)
            return w_msg(w_ref(dy, j, 0), slot(d, k, j), yr if d == 0 else yl)

        def y_wait(d, k, j):
            dy = -k if d == 0 else k
            w_msg(w_ref(dy, j, 0), slot(d, k, j), yr if d == 0 else yl).wait_recv()

        def y_both(j):
            y_msg(0, 1, j).start()
            y_msg(1, 1, j).start()

        w_msg(w_ref(0, 0, 0), 0, xr).start()
        w_msg(w_ref(0, 0, 0), 1, xl).start()
        y_both(0)
        z_start()
        w_msg(w_ref(0, 1, 0), 1, xl).wait_recv()
        w_msg(w_ref(0, 1, 0, 1), 3, xl).start()
        y_both(1)
        w_msg(w_ref(0, -1, 0), 0, xr).wait_recv()
        w_msg(w_ref(0, -1, 0, 0), 2, xr).start()
        y_both(3)
        z_tick(0)
        w_msg(w_ref(0, -2, 0, 0), 2, xr).wait_recv()
        w_msg(w_ref(0, 2, 0, 1), 3, xl).wait_recv()
        y_both(2)
        sib_msg(0, 0).start()

        events = []
        for k in range(1, 5):
            for j in X_ORDER:
                todo = [d for d in (0, 1) if has(d, k, j)]
                events.append((k, j, todo))
        merged = [[e] for e in events[:12]]
        merged.append([events[12], events[14]])
        merged.append([events[13], events[15]])
        for i in range(14):
            if i > 0:
                z_tick(i)
            for k, j, todo in merged[i]:
                for d in todo:
                    y_wait(d, k, j)
                    if has(d, k + 1, j):
                        y_msg(d, k + 1, j).start()
            if i in (3, 7, 11):
                k = (i + 1) // 4
                sib_msg(-k, 0).start()
                sib_msg(k, 0).start()
        sib_msg(4, 0).start()

        for i in range(4):
            dx, half, dev = ((0, None, xr), (0, None, xl), (-1, 0, xr), (1, 1, xl))[i]
            w_msg(w_ref(0, dx, 0, half), i, dev).wait_send()
        for k in range(1, 5):
            for j in range(4):
                for d in (0, 1):
                    if has(d, k, j):
                        y_msg(d, k, j).wait_send()

    def core1():
        def y_msg(d, k):
            dy = (1 - k) if d == 0 else (k - 1)
            half = None if k < 4 else d
            return w_msg(w_ref(dy, 0, 1, half), d * 5 + k, yr if d == 0 else yl)

        def y_wait(d, k):
            dy = -k if d == 0 else k
            half = None if k < 4 else d
            w_msg(w_ref(dy, 0, 1, half), d * 5 + k, yr if d == 0 else yl).wait_recv()

        def x_first(m):
            i = 10 + (m % NY) * 4
            return [w_msg(w_ref(m, 0, 1), i, xr), w_msg(w_ref(m, 0, 1), i + 1, xl)]

        def x_second(m, d):
            i = 10 + (m % NY) * 4
            return w_msg(w_ref(m, 2 * d - 1, 1, d), i + 2 + d, xl if d else xr)

        def x_send(m):
            for msg in x_first(m):
                msg.start()

        def x_mid(m):
            i = 10 + (m % NY) * 4
            w_msg(w_ref(m, -1, 1), i, xr).wait_recv()
            x_second(m, 0).start()
            w_msg(w_ref(m, 1, 1), i + 1, xl).wait_recv()
            x_second(m, 1).start()

        def x_end(m):
            i = 10 + (m % NY) * 4
            w_msg(w_ref(m, -2, 1, 0), i + 2, xr).wait_recv()
            w_msg(w_ref(m, 2, 1, 1), i + 3, xl).wait_recv()
            sib_msg(m, 1).start()

        def y_event(k):
            for d in (0, 1):
                y_wait(d, k)
                if k < 4:
                    y_msg(d, k + 1).start()
                    x_send(-k if d == 0 else k)
            if k == 4:
                x_send(4)

        y_msg(0, 1).start()
        y_msg(1, 1).start()
        x_send(0)
        z_start()
        plan = [
            lambda: x_mid(0), lambda: y_event(1), lambda: x_end(0), lambda: (x_mid(-1), x_mid(1)),
            lambda: y_event(2), lambda: (x_end(-1), x_end(1)), lambda: (x_mid(-2), x_mid(2)),
            lambda: y_event(3), lambda: (x_end(-2), x_end(2)), lambda: (x_mid(-3), x_mid(3)),
            lambda: y_event(4), lambda: (x_end(-3), x_end(3)), lambda: x_mid(4), lambda: x_end(4),
        ]
        for i in range(14):
            plan[i]()
            z_tick(i)
        for d in (0, 1):
            for k in range(1, 5):
                y_msg(d, k).wait_send()
        for m in range(NY):
            for msg in x_first(m) + [x_second(m, 0), x_second(m, 1)]:
                msg.wait_send()

    pl.when(c == 0)(core0)
    pl.when(c == 1)(core1)

    for m in range(NY):
        ref = wts.at[n_y(m), :, 1 - c]
        same(ref, s_send.at[m], s_recv.at[m], sib).wait_recv()
    for m in range(NY):
        sib_msg(m, c).wait_send()
    for pair in [(d, k, s) for d in (0, 1) for k in range(1, HALF + 1) for s in range(SUBS)]:
        if z_has(*pair):
            z_msg(*pair).wait_send()

    acc[...] = jnp.zeros_like(acc)

    @pl.loop(0, NZ)
    def _(f):
        acc[...] += nn(act[f], wts[f].reshape(FEAT, WCOLS))

    qkv[...] = acc[...].astype(BF16)
    head = lambda h: pl.ds(h * HD, HD)
    k_val, v_val = qkv[:, 512:640], qkv[:, 640:768]
    factor = HD ** -0.5
    kv = tn(k_val, v_val)
    gs = tn(qkv[:, head(0)], g_ref[:, head(0)])
    for h in range(1, GROUP):
        gs += tn(qkv[:, head(h)], g_ref[:, head(h)])
    st[:, 0] = kv.astype(BF16).reshape(ROW, HD // ROW, HD)
    st[:, 1] = (factor * gs).astype(BF16).reshape(ROW, HD // ROW, HD)

    def e1(d):
        return copy(st.at[n_r(d)], in1.at[r], e_send.at[0, d], e_recv.at[0, d], row_peer(d))

    def e1_wait(d):
        copy(st.at[r], in1.at[n_r(-d)], e_send.at[0, d], e_recv.at[0, d], row_peer(d)).wait_recv()

    for d in range(1, ROW):
        e1(d).start()
    in1[r] = st[r]
    rows_t = lax.broadcasted_iota(jnp.int32, (TOK, TOK), 0)
    cols_s = lax.broadcasted_iota(jnp.int32, (TOK, TOK), 1)
    causal = rows_t >= cols_s

    def attend(h):
        q_h, g_h = qkv[:, head(h)], g_ref[:, head(h)]
        k_v, v_v = qkv[:, 512:640], qkv[:, 640:768]
        s = jnp.where(causal, nt(q_h, k_v), 0.0).astype(BF16)
        gsc = jnp.where(causal, nt(g_h, v_v), 0.0).astype(BF16)
        dq[:, head(h)] = nn(gsc, k_v)
        if h == 0:
            dk[...] = tn(gsc, q_h)
            dv[...] = tn(s, g_h)
        else:
            dk[...] += tn(gsc, q_h)
            dv[...] += tn(s, g_h)

    attend(0)
    for d in range(1, ROW):
        e1_wait(d)
    pieces = [in1[i].astype(F32) for i in range(ROW)]
    total = pieces[0]
    for i in range(1, ROW):
        total = total + pieces[i]
    tot[...] = total.astype(BF16)

    def e2(d):
        return copy(tot, in2.at[y], e_send.at[1, d], e_recv.at[1, d], {"y": n_y(d)})

    def e2_wait(d):
        copy(tot, in2.at[n_y(-d)], e_send.at[1, d], e_recv.at[1, d], {"y": n_y(d)}).wait_recv()

    for d in range(1, NY):
        e2(d).start()
    in2[y] = tot[...]
    attend(1)
    attend(2)
    for d in range(1, NY):
        e2_wait(d)
    before = jnp.zeros((HD // ROW, HD), F32)
    after = jnp.zeros((HD // ROW, HD), F32)
    for i in range(NY):
        one = in2[i].astype(F32)
        before = before + jnp.where(i < y, one[0], 0.0)
        after = after + jnp.where(i > y, one[1], 0.0)
    for i in range(ROW):
        out3[i, 0] = before.astype(BF16)
        before = before + pieces[i][0]
    for i in reversed(range(ROW)):
        out3[i, 1] = after.astype(BF16)
        after = after + pieces[i][1]

    def e3(d):
        return copy(out3.at[n_r(d)], in3.at[r], e_send.at[2, d], e_recv.at[2, d], row_peer(d))

    def e3_wait(d):
        copy(out3.at[r], in3.at[n_r(-d)], e_send.at[2, d], e_recv.at[2, d], row_peer(d)).wait_recv()

    for d in range(1, ROW):
        e3(d).start()
    in3[r] = out3[r]
    attend(3)
    for d in range(1, ROW):
        e3_wait(d)
    for d in range(1, ROW):
        e1(d).wait_send()
        e2(d).wait_send()
        e3(d).wait_send()
    prefix = in3[:, 0].reshape(HD, HD)
    suffix = in3[:, 1].reshape(HD, HD)
    for h in range(GROUP):
        cross = nt(g_ref[:, head(h)], prefix)
        grads[:, head(h)] = (factor * (dq[:, head(h)] + cross)).astype(BF16)
    grads[:, 512:640] = (factor * dk[...] + nt(qkv[:, 640:768], suffix)).astype(BF16)
    grads[:, 640:768] = (factor * dv[...] + nn(qkv[:, 512:640], suffix)).astype(BF16)

    def share(dz, slot):
        part[slot] = nt(grads[...], wts[n_z(dz)].reshape(FEAT, WCOLS))

    def r_msg(d, k, s):
        ds = pl.ds(s * SUB, SUB)
        return copy(tx.at[d, k - 1, ds], rx.at[d, k - 1, ds], r_send.at[d, k, s], r_recv.at[d, k, s], zr if d == 0 else zl)

    def r_step(d, k, s):
        ds = pl.ds(s * SUB, SUB)
        value = part[d, ds]
        if z_has(d, k + 1, s):
            r_msg(d, k + 1, s).wait_recv()
            value = value + rx[d, k, ds].astype(F32)
        tx[d, k - 1, ds] = value.astype(BF16)
        r_msg(d, k, s).start()

    share(HALF, 0)
    for d in (0, 1):
        for s in (R_LAST if d == 0 else L_LAST):
            ds = pl.ds(s * SUB, SUB)
            tx[d, HALF - 1, ds] = part[0, ds].astype(BF16)
            r_msg(d, HALF, s).start()
    for k in range(HALF - 1, 0, -1):
        share(k, 0)
        share(-k, 1)
        for i in range(SUBS):
            r_step(0, k, L_ORDER[i])
            r_step(1, k, R_ORDER[i])
    share(0, 0)
    for i in range(SUBS):
        s = L_ORDER[i]
        ds = pl.ds(s * SUB, SUB)
        r_msg(0, 1, s).wait_recv()
        r_msg(1, 1, s).wait_recv()
        o_ref[ds] = (part[0, ds] + rx[0, 0, ds].astype(F32) + rx[1, 0, ds].astype(F32)).astype(BF16)
    for d in (0, 1):
        for k in range(1, HALF + 1):
            for s in range(SUBS):
                if z_has(d, k, s):
                    r_msg(d, k, s).wait_send()


def local(activations, grad_out, query_weight, key_weight, value_weight):
    dma = pltpu.SemaphoreType.DMA
    return pl.pallas_call(
        kernel,
        out_shape=jax.ShapeDtypeStruct((TOK, FEAT), BF16),
        in_specs=[pl.BlockSpec(memory_space=pltpu.VMEM)] * 5,
        out_specs=pl.BlockSpec(memory_space=pltpu.VMEM),
        scratch_shapes=[
            pltpu.VMEM((NZ, TOK, FEAT), BF16),
            pltpu.VMEM((NY, NX, NC, WROWS, WCOLS), BF16),
            pltpu.VMEM((TOK, WCOLS), F32),
            pltpu.VMEM((TOK, WCOLS), BF16),
            pltpu.VMEM((TOK, FEAT), F32),
            pltpu.VMEM((TOK, HD), F32),
            pltpu.VMEM((TOK, HD), F32),
            pltpu.VMEM((TOK, WCOLS), BF16),
            pltpu.VMEM((2, TOK, FEAT), F32),
            pltpu.VMEM((2, HALF, TOK, FEAT), BF16),
            pltpu.VMEM((2, HALF, TOK, FEAT), BF16),
            pltpu.VMEM((ROW, 2, HD // ROW, HD), BF16),
            pltpu.VMEM((ROW, 2, HD // ROW, HD), BF16),
            pltpu.VMEM((2, HD // ROW, HD), BF16),
            pltpu.VMEM((NY, 2, HD // ROW, HD), BF16),
            pltpu.VMEM((ROW, 2, HD // ROW, HD), BF16),
            pltpu.VMEM((ROW, 2, HD // ROW, HD), BF16),
            dma((2, HALF + 1, SUBS)),
            dma((2, HALF + 1, SUBS)),
            dma((44,)),
            dma((44,)),
            dma((NY,)),
            dma((NY,)),
            dma((3, 8)),
            dma((3, 8)),
            dma((2, HALF + 1, SUBS)),
            dma((2, HALF + 1, SUBS)),
        ],
        compiler_params=pltpu.CompilerParams(
            collective_id=0, has_side_effects=True, vmem_limit_bytes=48 * 1024 * 1024
        ),
        cost_estimate=pl.CostEstimate(flops=4_000_000_000, bytes_accessed=2_000_000, transcendentals=0),
    )(activations, grad_out, query_weight, key_weight, value_weight)


def solution(mesh):
    finer = Mesh(mesh.devices.reshape(NY, NX, NC, NZ), AXES)
    spec = P(SEQ, "head")
    return jax.shard_map(
        local, mesh=finer, in_specs=(spec,) * 5, out_specs=spec, check_vma=False
    )
```

time: 255 us -> 88.2 us (0.35); the launches traced: 251 us -> 87.9 us
  waiting for transfers between devices: 128 us -> 0 us
  Pallas kernels: 0 us -> 83 us
  blocking collectives: 68.5 us -> 0 us
  matrix products: 25 us -> 0 us
  between operations: 13.6 us -> 0.01 us
  starting transfers between devices: 10.9 us -> 0 us
    pallas_call x0 -> x1, Pallas kernels: none -> 83 us  [local(): pl.pallas_call(kernel, out_shape=jax.ShapeDtypeStruct((TOK, FEAT), BF16),...]
    all_gather x6 -> x0, blocking collectives: 68.5 us -> none  [entering(): pieces = lax.all_gather(so_far.astype(jnp.bfloat16), axis)]
    all_to_all x1 -> x0, waiting for transfers between devices: 48.3 us -> none  [from_everyone(): return lax.all_to_all(copies, axis, split_axis=0, concat_axis=0, tiled=True)]
    reduce_scatter x1 -> x0, waiting for transfers between devices: 46.9 us -> none  [local(): lax.psum_scatter(partial_input.astype(jnp.bfloat16), 'head', scatter_dime...]
    all_gather x1 -> x0, waiting for transfers between devices: 33 us -> none  [in_one_piece(): out, at, done = (lax.all_gather(both, axis, axis=dim, tiled=True), 0, [])]
    dot_general x14 -> x0, matrix products: 25 us -> none  [the longest x3 16.1 us: contract_rows(): lax.dot_general(grads, weight, (((1,), (1,)), ((), ())), preferred_elemen...]
    all_to_all x1 -> x0, starting transfers between devices: 10.9 us -> none  [from_everyone(): return lax.all_to_all(copies, axis, split_axis=0, concat_axis=0, tiled=True)]
    unnamed x3 -> x11, local copies, waits for them, and re-layouts: 1.09 us -> 4.88 us
  transfers between devices with their start and end apart: 3 -> 0, of which waited for: 3 -> 0; matrix products, arithmetic and copies ran while one was open for 1% -> 0% of each run, Pallas kernels for 0% -> 0%
where the time goes in v1:
time: 88.2 us; the launch traced here: 87.9 us
  Pallas kernels  83 us (94%)
  local copies, waits for them, and re-layouts  4.88 us (6%)
    pallas_call x1, Pallas kernels, local(): pl.pallas_call(kernel, out_shape=jax.ShapeDtypeStruct((TOK, FEAT), BF16),...  83 us
    unnamed x11, local copies, waits for them, and re-layouts  4.88 us

profile of v1, /device:TPU:1, one launch (start us, length us, event | category | flops | bytes accessed | tf_op | source)
XLA Modules:
  0.0 87.9 jit_solution(17819417311633707394)
XLA Ops:
  0.0 0.0 copy-start
  0.0 0.9 %copy-done = bf16[256,512]{1,0:T(8,128)(2,1)S(1)} copy-done((bf16[256,512]{1,0:T(8,128)(2,1)S(1)}, bf16[256,512]{1,0:T(8,128)(2,1)}, u32[]{:S(2)}) %copy-start) | copy-done | bytes 262168
  1.0 0.0 copy-start.1
  1.0 0.9 %copy-done.1 = bf16[256,512]{1,0:T(8,128)(2,1)S(1)} copy-done((bf16[256,512]{1,0:T(8,128)(2,1)S(1)}, bf16[256,512]{1,0:T(8,128)(2,1)}, u32[]{:S(2)}) %copy-start.1) | copy-done | bytes 262168
  1.9 0.0 copy-start.2
  1.9 0.8 copy-done.2
  2.7 0.0 copy-start.3
  2.7 0.7 copy-done.3
  3.5 0.0 copy-start.4
  3.5 0.7 copy-done.4
  4.2 83.0 %shard_map.55 = bf16[256,512]{1,0:T(8,128)(2,1)S(1)} custom-call(bf16[256,512]{1,0:T(8,128)(2,1)S(1)} %copy-done, bf16[256,512]{1,0:T(8,128)(2,1)S(1)} %copy-done.1, bf16[64,512]{1,0:T(8,128)(2,1)S(1)} %copy-done.2, bf16[64,128]{1,0:T(8,128)(2,1)S(1)} %copy-done.3, bf16[64,128]{1,0:T(8,128)(2,1)S(1)} %copy-done.4), custom_call_target="tpu_custom_call" | custom-call | flops 4000000000 | bytes 2000000 | tf_op jit(solution)/shard_map/pallas_call | solution.py:416
  87.2 0.7 copy.7
Async XLA Ops:
  0.0 0.9 %copy-start = (bf16[256,512]{1,0:T(8,128)(2,1)S(1)}, bf16[256,512]{1,0:T(8,128)(2,1)}, u32[]{:S(2)}) copy-start(bf16[256,512]{1,0:T(8,128)(2,1)} %a_ref.1) | copy-start | bytes 786436
  1.0 0.9 %copy-start.1 = (bf16[256,512]{1,0:T(8,128)(2,1)S(1)}, bf16[256,512]{1,0:T(8,128)(2,1)}, u32[]{:S(2)}) copy-start(bf16[256,512]{1,0:T(8,128)(2,1)} %g_ref.1) | copy-start | bytes 786436
  1.9 0.8 copy-start.2
  2.7 0.7 copy-start.3
  3.5 0.7 copy-start.4

commit v2 on v1

--- a/solution.py
+++ b/solution.py
@@ -23,6 +23,28 @@
 SUBS = 4
 SUB = TOK // SUBS
 HALF = NZ // 2
+CUT = 64
+REST = NC * WROWS - CUT
+
+
+def halves(start, rows):
+    first = (rows // 2 + 15) // 16 * 16
+    return ((start, first), (start + first, rows - first))
+
+
+CORE0 = (
+    "near", (1, 0), 0, "far", 1, (1, 1), (1, 3), (2, 0), 2, 3, (1, 2), (2, 1), (2, 3), 4, (3, 0), 5,
+    (2, 2), (3, 1), 6, (3, 3), 7, (4, 0), 8, (3, 2), 9, (4, 1), (4, 3), 10, (4, 2), 11,
+)
+CORE1 = (
+    "y1", 0, "m0", 1, "y2", 2, "m-1", "m1", "e0", 3, "y3", 4, "e-1", "e1", "m-2", "m2", 5, 6,
+    "y4", 7, "e-2", "e2", "m-3", "m3", 8, 9, "e-3", "e3", "m4", 10, 11, "e4",
+)
+FAR_FIRST = (4, 3, 5, 2, 6, 1, 7)
+PARTS = (
+    ((0, CUT),) + halves(0, CUT),
+    ((CUT, REST),) + halves(CUT, REST),
+)
 R_ORDER = (0, 1, 2, 3)
 L_ORDER = (2, 3, 0, 1)
 R_LAST = (0, 1)
@@ -45,10 +67,10 @@
 
 
 def kernel(
-    a_ref, g_ref, wq_ref, wk_ref, wv_ref, o_ref,
+    a_ref, go_ref, wq_ref, wk_ref, wv_ref, o_ref,
     act, wts, acc, qkv, dq, dk, dv, grads, part, tx, rx,
     st, in1, tot, in2, out3, in3,
-    z_send, z_recv, w_send, w_recv, s_send, s_recv, e_send, e_recv, r_send, r_recv,
+    g_ref, o_buf, i_sem, z_send, z_recv, w_send, w_recv, s_send, s_recv, e_send, e_recv, r_send, r_recv,
 ):
     y, x, c, z = (lax.axis_index(n) for n in AXES)
     r = x * NC + c
@@ -67,10 +89,18 @@
     for peer in peers:
         pl.semaphore_signal(barrier, inc=1, device_id=peer, device_id_type=pl.DeviceIdType.MESH)
 
-    act[z] = a_ref[...]
-    wts[y, x, c, :, 0:512] = wq_ref[...]
-    wts[y, x, c, :, 512:640] = wk_ref[...]
-    wts[y, x, c, :, 640:768] = wv_ref[...]
+    own = pl.ds(pl.multiple_of(c * WROWS, WROWS), WROWS)
+    loads = [
+        pltpu.make_async_copy(a_ref, act.at[z], i_sem.at[0]),
+        pltpu.make_async_copy(wq_ref, wts.at[y, x, own, pl.ds(0, 512)], i_sem.at[1]),
+        pltpu.make_async_copy(wk_ref, wts.at[y, x, own, pl.ds(512, 128)], i_sem.at[2]),
+        pltpu.make_async_copy(wv_ref, wts.at[y, x, own, pl.ds(640, 128)], i_sem.at[3]),
+        pltpu.make_async_copy(go_ref, g_ref, i_sem.at[4]),
+    ]
+    for load in loads:
+        load.start()
+    for load in loads:
+        load.wait()
     pl.semaphore_wait(barrier, len(peers))
 
     def copy(src, dst, ssem, rsem, dev):
@@ -115,15 +145,21 @@
                 z_msg(d, k + 1, s).start()
 
     def w_ref(dy, dx, core, half=None):
-        ref = wts.at[n_y(dy), n_x(dx), core]
-        return ref if half is None else ref.at[pl.ds(32 * half, 32)]
+        first, rows = PARTS[core][0 if half is None else 1 + half]
+        return wts.at[n_y(dy), n_x(dx), pl.ds(first, rows)]
 
     def w_msg(ref, i, dev):
         return same(ref, w_send.at[i], w_recv.at[i], dev)
 
+    def sib_ref(m, core):
+        return wts.at[n_y(m), :, pl.ds(PARTS[core][0][0], PARTS[core][0][1])]
+
     def sib_msg(m, core):
-        ref = wts.at[n_y(m), :, core]
-        return same(ref, s_send.at[m % NY], s_recv.at[m % NY], sib)
+        return same(sib_ref(m, core), s_send.at[m % NY], s_recv.at[m % NY], sib)
+
+    def lend_msg():
+        ref = wts.at[y, x, pl.ds(CUT, WROWS - CUT)]
+        return same(ref, s_send.at[NY], s_recv.at[NY], sib)
 
     def core0():
         slot = lambda d, k, j: 4 + (d * 5 + k) * 4 + j
@@ -143,44 +179,48 @@
             y_msg(0, 1, j).start()
             y_msg(1, 1, j).start()
 
+        def x_near():
+            w_msg(w_ref(0, 1, 0), 1, xl).wait_recv()
+            w_msg(w_ref(0, 1, 0, 1), 3, xl).start()
+            y_both(1)
+            w_msg(w_ref(0, -1, 0), 0, xr).wait_recv()
+            w_msg(w_ref(0, -1, 0, 0), 2, xr).start()
+            y_both(3)
+
+        def x_far():
+            w_msg(w_ref(0, -2, 0, 0), 2, xr).wait_recv()
+            w_msg(w_ref(0, 2, 0, 1), 3, xl).wait_recv()
+            y_both(2)
+            sib_msg(0, 0).start()
+
+        def y_event(k, j):
+            for d in (0, 1):
+                if has(d, k, j):
+                    y_wait(d, k, j)
+                    if has(d, k + 1, j):
+                        y_msg(d, k + 1, j).start()
+            if j == 2:
+                for m in (-k, k) if k < 4 else (4,):
+                    sib_msg(m, 0).start()
+
+        if CUT < WROWS:
+            lend_msg().start()
         w_msg(w_ref(0, 0, 0), 0, xr).start()
         w_msg(w_ref(0, 0, 0), 1, xl).start()
         y_both(0)
         z_start()
-        w_msg(w_ref(0, 1, 0), 1, xl).wait_recv()
-        w_msg(w_ref(0, 1, 0, 1), 3, xl).start()
-        y_both(1)
-        w_msg(w_ref(0, -1, 0), 0, xr).wait_recv()
-        w_msg(w_ref(0, -1, 0, 0), 2, xr).start()
-        y_both(3)
-        z_tick(0)
-        w_msg(w_ref(0, -2, 0, 0), 2, xr).wait_recv()
-        w_msg(w_ref(0, 2, 0, 1), 3, xl).wait_recv()
-        y_both(2)
-        sib_msg(0, 0).start()
-
-        events = []
-        for k in range(1, 5):
-            for j in X_ORDER:
-                todo = [d for d in (0, 1) if has(d, k, j)]
-                events.append((k, j, todo))
-        merged = [[e] for e in events[:12]]
-        merged.append([events[12], events[14]])
-        merged.append([events[13], events[15]])
-        for i in range(14):
-            if i > 0:
-                z_tick(i)
-            for k, j, todo in merged[i]:
-                for d in todo:
-                    y_wait(d, k, j)
-                    if has(d, k + 1, j):
-                        y_msg(d, k + 1, j).start()
-            if i in (3, 7, 11):
-                k = (i + 1) // 4
-                sib_msg(-k, 0).start()
-                sib_msg(k, 0).start()
-        sib_msg(4, 0).start()
-
+        for step in CORE0:
+            if step == "near":
+                x_near()
+            elif step == "far":
+                x_far()
+            elif isinstance(step, int):
+                z_tick(step)
+            else:
+                y_event(*step)
+
+        if CUT < WROWS:
+            lend_msg().wait_send()
         for i in range(4):
             dx, half, dev = ((0, None, xr), (0, None, xl), (-1, 0, xr), (1, 1, xl))[i]
             w_msg(w_ref(0, dx, 0, half), i, dev).wait_send()
@@ -235,19 +275,17 @@
             if k == 4:
                 x_send(4)
 
+        z_start()
+        if CUT < WROWS:
+            lend_msg().wait_recv()
         y_msg(0, 1).start()
         y_msg(1, 1).start()
         x_send(0)
-        z_start()
-        plan = [
-            lambda: x_mid(0), lambda: y_event(1), lambda: x_end(0), lambda: (x_mid(-1), x_mid(1)),
-            lambda: y_event(2), lambda: (x_end(-1), x_end(1)), lambda: (x_mid(-2), x_mid(2)),
-            lambda: y_event(3), lambda: (x_end(-2), x_end(2)), lambda: (x_mid(-3), x_mid(3)),
-            lambda: y_event(4), lambda: (x_end(-3), x_end(3)), lambda: x_mid(4), lambda: x_end(4),
-        ]
-        for i in range(14):
-            plan[i]()
-            z_tick(i)
+        for step in CORE1:
+            if isinstance(step, int):
+                z_tick(step)
+            else:
+                (y_event, x_mid, x_end)["yme".index(step[0])](int(step[1:]))
         for d in (0, 1):
             for k in range(1, 5):
                 y_msg(d, k).wait_send()
@@ -258,20 +296,47 @@
     pl.when(c == 0)(core0)
     pl.when(c == 1)(core1)
 
+    def sib_wait(m):
+        def wait_for(core):
+            same(sib_ref(m, core), s_send.at[m], s_recv.at[m], sib).wait_recv()
+
+        pl.when(c == 0)(lambda: wait_for(1))
+        pl.when(c == 1)(lambda: wait_for(0))
+
+    def sib_sent(m):
+        pl.when(c == 0)(lambda: sib_msg(m, 0).wait_send())
+        pl.when(c == 1)(lambda: sib_msg(m, 1).wait_send())
+
+    far_y, far_z = n_y(4), n_z(4)
+
+    def project(f):
+        acc[...] += nn(act[f], wts[f].reshape(FEAT, WCOLS))
+
+    acc[...] = jnp.zeros_like(acc)
     for m in range(NY):
-        ref = wts.at[n_y(m), :, 1 - c]
-        same(ref, s_send.at[m], s_recv.at[m], sib).wait_recv()
+        if m != 4:
+            sib_wait(m)
+
+    @pl.loop(0, NZ)
+    def _(f):
+        @pl.when(jnp.logical_and(f != far_y, f != far_z))
+        def _():
+            project(f)
+
+    z_tick(12)
+    z_tick(13)
+    sib_wait(4)
+    project(far_y)
+
+    @pl.when(far_y != far_z)
+    def _():
+        project(far_z)
+
     for m in range(NY):
-        sib_msg(m, c).wait_send()
+        sib_sent(m)
     for pair in [(d, k, s) for d in (0, 1) for k in range(1, HALF + 1) for s in range(SUBS)]:
         if z_has(*pair):
             z_msg(*pair).wait_send()
-
-    acc[...] = jnp.zeros_like(acc)
-
-    @pl.loop(0, NZ)
-    def _(f):
-        acc[...] += nn(act[f], wts[f].reshape(FEAT, WCOLS))
 
     qkv[...] = acc[...].astype(BF16)
     head = lambda h: pl.ds(h * HD, HD)
@@ -290,7 +355,7 @@
     def e1_wait(d):
         copy(st.at[r], in1.at[n_r(-d)], e_send.at[0, d], e_recv.at[0, d], row_peer(d)).wait_recv()
 
-    for d in range(1, ROW):
+    for d in FAR_FIRST:
         e1(d).start()
     in1[r] = st[r]
     rows_t = lax.broadcasted_iota(jnp.int32, (TOK, TOK), 0)
@@ -320,14 +385,16 @@
     tot[...] = total.astype(BF16)
 
     def e2(d):
-        return copy(tot, in2.at[y], e_send.at[1, d], e_recv.at[1, d], {"y": n_y(d)})
+        kind = jnp.where(y + d < NY, 0, 1)
+        return copy(tot.at[kind], in2.at[y, kind], e_send.at[1, d], e_recv.at[1, d], {"y": n_y(d)})
 
     def e2_wait(d):
-        copy(tot, in2.at[n_y(-d)], e_send.at[1, d], e_recv.at[1, d], {"y": n_y(d)}).wait_recv()
-
-    for d in range(1, NY):
+        kind = jnp.where(y - d >= 0, 0, 1)
+        copy(tot.at[kind], in2.at[n_y(-d), kind], e_send.at[1, d], e_recv.at[1, d], {"y": n_y(d)}).wait_recv()
+
+    for d in FAR_FIRST:
         e2(d).start()
-    in2[y] = tot[...]
+    in2[y] = jnp.zeros_like(tot)
     attend(1)
     attend(2)
     for d in range(1, NY):
@@ -335,9 +402,9 @@
     before = jnp.zeros((HD // ROW, HD), F32)
     after = jnp.zeros((HD // ROW, HD), F32)
     for i in range(NY):
-        one = in2[i].astype(F32)
-        before = before + jnp.where(i < y, one[0], 0.0)
-        after = after + jnp.where(i > y, one[1], 0.0)
+        one = in2[i, jnp.where(i < y, 0, 1)].astype(F32)
+        before = before + jnp.where(i < y, one, 0.0)
+        after = after + jnp.where(i > y, one, 0.0)
     for i in range(ROW):
         out3[i, 0] = before.astype(BF16)
         before = before + pieces[i][0]
@@ -351,7 +418,7 @@
     def e3_wait(d):
         copy(out3.at[r], in3.at[n_r(-d)], e_send.at[2, d], e_recv.at[2, d], row_peer(d)).wait_recv()
 
-    for d in range(1, ROW):
+    for d in FAR_FIRST:
         e3(d).start()
     in3[r] = out3[r]
     attend(3)
@@ -398,12 +465,21 @@
             r_step(0, k, L_ORDER[i])
             r_step(1, k, R_ORDER[i])
     share(0, 0)
+
+    def out_copy(s):
+        ds = pl.ds(s * SUB, SUB)
+        return pltpu.make_async_copy(o_buf.at[ds], o_ref.at[ds], i_sem.at[5 + s])
+
     for i in range(SUBS):
         s = L_ORDER[i]
         ds = pl.ds(s * SUB, SUB)
         r_msg(0, 1, s).wait_recv()
         r_msg(1, 1, s).wait_recv()
-        o_ref[ds] = (part[0, ds] + rx[0, 0, ds].astype(F32) + rx[1, 0, ds].astype(F32)).astype(BF16)
+        total = part[0, ds] + rx[0, 0, ds].astype(F32) + rx[1, 0, ds].astype(F32)
+        o_buf[ds] = total.astype(BF16)
+        out_copy(s).start()
+    for s in range(SUBS):
+        out_copy(s).wait()
     for d in (0, 1):
         for k in range(1, HALF + 1):
             for s in range(SUBS):
@@ -416,11 +492,11 @@
     return pl.pallas_call(
         kernel,
         out_shape=jax.ShapeDtypeStruct((TOK, FEAT), BF16),
-        in_specs=[pl.BlockSpec(memory_space=pltpu.VMEM)] * 5,
-        out_specs=pl.BlockSpec(memory_space=pltpu.VMEM),
+        in_specs=[pl.BlockSpec(memory_space=pltpu.HBM)] * 5,
+        out_specs=pl.BlockSpec(memory_space=pltpu.HBM),
         scratch_shapes=[
             pltpu.VMEM((NZ, TOK, FEAT), BF16),
-            pltpu.VMEM((NY, NX, NC, WROWS, WCOLS), BF16),
+            pltpu.VMEM((NY, NX, NC * WROWS, WCOLS), BF16),
             pltpu.VMEM((TOK, WCOLS), F32),
             pltpu.VMEM((TOK, WCOLS), BF16),
             pltpu.VMEM((TOK, FEAT), F32),
@@ -436,19 +512,22 @@
             pltpu.VMEM((NY, 2, HD // ROW, HD), BF16),
             pltpu.VMEM((ROW, 2, HD // ROW, HD), BF16),
             pltpu.VMEM((ROW, 2, HD // ROW, HD), BF16),
+            pltpu.VMEM((TOK, FEAT), BF16),
+            pltpu.VMEM((TOK, FEAT), BF16),
+            dma((5 + SUBS,)),
             dma((2, HALF + 1, SUBS)),
             dma((2, HALF + 1, SUBS)),
             dma((44,)),
             dma((44,)),
-            dma((NY,)),
-            dma((NY,)),
+            dma((NY + 1,)),
+            dma((NY + 1,)),
             dma((3, 8)),
             dma((3, 8)),
             dma((2, HALF + 1, SUBS)),
             dma((2, HALF + 1, SUBS)),
         ],
         compiler_params=pltpu.CompilerParams(
-            collective_id=0, has_side_effects=True, vmem_limit_bytes=48 * 1024 * 1024
+            collective_id=0, has_side_effects=True, vmem_limit_bytes=62 * 1024 * 1024
         ),
         cost_estimate=pl.CostEstimate(flops=4_000_000_000, bytes_accessed=2_000_000, transcendentals=0),
     )(activations, grad_out, query_weight, key_weight, value_weight)

time: 88.2 us -> 83 us (0.941)
  local copies, waits for them, and re-layouts: 4.88 us -> 1.67 us
  Pallas kernels: 83 us -> 81.1 us
    unnamed x11 -> x1, local copies, waits for them, and re-layouts: 4.88 us -> 1.67 us
    pallas_call x1, Pallas kernels: 83 us -> 81.1 us  [local(): pl.pallas_call(kernel, out_shape=jax.ShapeDtypeStruct((TOK, FEAT), BF16),...]
where the time goes in v2:
time: 83 us; the launch traced here: 82.8 us
  Pallas kernels  81.1 us (98%)
  local copies, waits for them, and re-layouts  1.67 us (2%)
    pallas_call x1, Pallas kernels, local(): pl.pallas_call(kernel, out_shape=jax.ShapeDtypeStruct((TOK, FEAT), BF16),...  81.1 us
    unnamed x1, local copies, waits for them, and re-layouts  1.67 us

profile of v2, /device:TPU:1, one launch (start us, length us, event | category | flops | bytes accessed | tf_op | source)
XLA Modules:
  0.0 82.8 jit_solution(17348985023646744044)
XLA Ops:
  0.0 81.1 %shard_map.55 = bf16[256,512]{1,0:T(8,128)(2,1)} custom-call(bf16[256,512]{1,0:T(8,128)(2,1)} %a_ref.1, bf16[256,512]{1,0:T(8,128)(2,1)} %go_ref.1, bf16[64,512]{1,0:T(8,128)(2,1)} %wq_ref.1, bf16[64,128]{1,0:T(8,128)(2,1)} %wk_ref.1, bf16[64,128]{1,0:T(8,128)(2,1)} %wv_ref.1), custom_call_target="tpu_custom_call" | custom-call | flops 4000000000 | bytes 2000000 | tf_op jit(solution)/shard_map/pallas_call | solution.py:492
  81.1 1.7 %copy.7 = bf16[256,512]{1,0:T(8,128)(2,1)} copy(bf16[256,512]{1,0:T(8,128)(2,1)} %shard_map.55) | data formatting | bytes 524288

commit v3 on v2

--- a/solution.py
+++ b/solution.py
@@ -40,6 +40,11 @@
     "y1", 0, "m0", 1, "y2", 2, "m-1", "m1", "e0", 3, "y3", 4, "e-1", "e1", "m-2", "m2", 5, 6,
     "y4", 7, "e-2", "e2", "m-3", "m3", 8, 9, "e-3", "e3", "m4", 10, 11, "e4",
 )
+PIECES = 2
+PIECE = TOK // PIECES
+R_TURN = tuple(range(PIECES))
+R_PART, L_PART = R_TURN[: PIECES // 2], R_TURN[PIECES // 2 :]
+L_TURN = L_PART + R_PART
 FAR_FIRST = (4, 3, 5, 2, 6, 1, 7)
 PARTS = (
     ((0, CUT),) + halves(0, CUT),
@@ -70,7 +75,7 @@
     a_ref, go_ref, wq_ref, wk_ref, wv_ref, o_ref,
     act, wts, acc, qkv, dq, dk, dv, grads, part, tx, rx,
     st, in1, tot, in2, out3, in3,
-    g_ref, o_buf, i_sem, z_send, z_recv, w_send, w_recv, s_send, s_recv, e_send, e_recv, r_send, r_recv,
+    g_ref, i_sem, z_send, z_recv, w_send, w_recv, s_send, s_recv, e_send, e_recv, r_send, r_recv,
 ):
     y, x, c, z = (lax.axis_index(n) for n in AXES)
     r = x * NC + c
@@ -84,11 +89,6 @@
     sib = {"core": 1 - c}
     row_peer = lambda d: {"x": n_r(d) // NC, "core": lax.rem(n_r(d), NC)}
 
-    barrier = pltpu.get_barrier_semaphore()
-    peers = [zr, zl] + [row_peer(d) for d in range(1, ROW)] + [{"y": n_y(d)} for d in range(1, NY)]
-    for peer in peers:
-        pl.semaphore_signal(barrier, inc=1, device_id=peer, device_id_type=pl.DeviceIdType.MESH)
-
     own = pl.ds(pl.multiple_of(c * WROWS, WROWS), WROWS)
     loads = [
         pltpu.make_async_copy(a_ref, act.at[z], i_sem.at[0]),
@@ -99,9 +99,14 @@
     ]
     for load in loads:
         load.start()
-    for load in loads:
+    barrier = pltpu.get_barrier_semaphore()
+    peers = [zr, zl] + [row_peer(d) for d in range(1, ROW)] + [{"y": n_y(d)} for d in range(1, NY)]
+    for peer in peers:
+        pl.semaphore_signal(barrier, inc=1, device_id=peer, device_id_type=pl.DeviceIdType.MESH)
+
+    pl.semaphore_wait(barrier, len(peers))
+    for load in loads[1:4]:
         load.wait()
-    pl.semaphore_wait(barrier, len(peers))
 
     def copy(src, dst, ssem, rsem, dev):
         return pltpu.make_async_remote_copy(
@@ -115,6 +120,11 @@
     def z_msg(d, k, s):
         origin = n_z(1 - k) if d == 0 else n_z(k - 1)
         ref = act.at[origin, pl.ds(s * SUB, SUB)]
+        if k == 1:
+            return copy(
+                a_ref.at[pl.ds(s * SUB, SUB)], ref, z_send.at[d, k, s], z_recv.at[d, k, s],
+                zr if d == 0 else zl,
+            )
         return same(ref, z_send.at[d, k, s], z_recv.at[d, k, s], zr if d == 0 else zl)
 
     def z_wait(d, k, s):
@@ -313,6 +323,8 @@
         acc[...] += nn(act[f], wts[f].reshape(FEAT, WCOLS))
 
     acc[...] = jnp.zeros_like(acc)
+    loads[0].wait()
+    loads[4].wait()
     for m in range(NY):
         if m != 4:
             sib_wait(m)
@@ -439,14 +451,17 @@
     def share(dz, slot):
         part[slot] = nt(grads[...], wts[n_z(dz)].reshape(FEAT, WCOLS))
 
+    def r_has(d, k, s):
+        return k < HALF or (k == HALF and s in (R_PART if d == 0 else L_PART))
+
     def r_msg(d, k, s):
-        ds = pl.ds(s * SUB, SUB)
+        ds = pl.ds(s * PIECE, PIECE)
         return copy(tx.at[d, k - 1, ds], rx.at[d, k - 1, ds], r_send.at[d, k, s], r_recv.at[d, k, s], zr if d == 0 else zl)
 
     def r_step(d, k, s):
-        ds = pl.ds(s * SUB, SUB)
+        ds = pl.ds(s * PIECE, PIECE)
         value = part[d, ds]
-        if z_has(d, k + 1, s):
+        if r_has(d, k + 1, s):
             r_msg(d, k + 1, s).wait_recv()
             value = value + rx[d, k, ds].astype(F32)
         tx[d, k - 1, ds] = value.astype(BF16)
@@ -454,46 +469,40 @@
 
     share(HALF, 0)
     for d in (0, 1):
-        for s in (R_LAST if d == 0 else L_LAST):
-            ds = pl.ds(s * SUB, SUB)
+        for s in (R_PART if d == 0 else L_PART):
+            ds = pl.ds(s * PIECE, PIECE)
             tx[d, HALF - 1, ds] = part[0, ds].astype(BF16)
             r_msg(d, HALF, s).start()
     for k in range(HALF - 1, 0, -1):
         share(k, 0)
         share(-k, 1)
-        for i in range(SUBS):
-            r_step(0, k, L_ORDER[i])
-            r_step(1, k, R_ORDER[i])
+        for i in range(PIECES):
+            r_step(0, k, L_TURN[i])
+            r_step(1, k, R_TURN[i])
     share(0, 0)
-
-    def out_copy(s):
-        ds = pl.ds(s * SUB, SUB)
-        return pltpu.make_async_copy(o_buf.at[ds], o_ref.at[ds], i_sem.at[5 + s])
-
-    for i in range(SUBS):
-        s = L_ORDER[i]
-        ds = pl.ds(s * SUB, SUB)
+    for i in range(PIECES):
+        s = L_TURN[i]
+        ds = pl.ds(s * PIECE, PIECE)
         r_msg(0, 1, s).wait_recv()
         r_msg(1, 1, s).wait_recv()
         total = part[0, ds] + rx[0, 0, ds].astype(F32) + rx[1, 0, ds].astype(F32)
-        o_buf[ds] = total.astype(BF16)
-        out_copy(s).start()
-    for s in range(SUBS):
-        out_copy(s).wait()
+        o_ref[ds] = total.astype(BF16)
     for d in (0, 1):
         for k in range(1, HALF + 1):
-            for s in range(SUBS):
-                if z_has(d, k, s):
+            for s in range(PIECES):
+                if r_has(d, k, s):
                     r_msg(d, k, s).wait_send()
 
 
 def local(activations, grad_out, query_weight, key_weight, value_weight):
     dma = pltpu.SemaphoreType.DMA
+    operands = (activations, grad_out, query_weight, key_weight, value_weight)
+    operands = [pltpu.with_memory_space_constraint(v, pltpu.HBM) for v in operands]
     return pl.pallas_call(
         kernel,
         out_shape=jax.ShapeDtypeStruct((TOK, FEAT), BF16),
         in_specs=[pl.BlockSpec(memory_space=pltpu.HBM)] * 5,
-        out_specs=pl.BlockSpec(memory_space=pltpu.HBM),
+        out_specs=pl.BlockSpec(memory_space=pltpu.VMEM),
         scratch_shapes=[
             pltpu.VMEM((NZ, TOK, FEAT), BF16),
             pltpu.VMEM((NY, NX, NC * WROWS, WCOLS), BF16),
@@ -503,7 +512,7 @@
             pltpu.VMEM((TOK, HD), F32),
             pltpu.VMEM((TOK, HD), F32),
             pltpu.VMEM((TOK, WCOLS), BF16),
-            pltpu.VMEM((2, TOK, FEAT), F32),
+            pltpu.VMEM((4, TOK, FEAT), F32),
             pltpu.VMEM((2, HALF, TOK, FEAT), BF16),
             pltpu.VMEM((2, HALF, TOK, FEAT), BF16),
             pltpu.VMEM((ROW, 2, HD // ROW, HD), BF16),
@@ -513,8 +522,7 @@
             pltpu.VMEM((ROW, 2, HD // ROW, HD), BF16),
             pltpu.VMEM((ROW, 2, HD // ROW, HD), BF16),
             pltpu.VMEM((TOK, FEAT), BF16),
-            pltpu.VMEM((TOK, FEAT), BF16),
-            dma((5 + SUBS,)),
+            dma((5,)),
             dma((2, HALF + 1, SUBS)),
             dma((2, HALF + 1, SUBS)),
             dma((44,)),
@@ -523,14 +531,14 @@
             dma((NY + 1,)),
             dma((3, 8)),
             dma((3, 8)),
-            dma((2, HALF + 1, SUBS)),
-            dma((2, HALF + 1, SUBS)),
+            dma((2, HALF + 1, PIECES)),
+            dma((2, HALF + 1, PIECES)),
         ],
         compiler_params=pltpu.CompilerParams(
-            collective_id=0, has_side_effects=True, vmem_limit_bytes=62 * 1024 * 1024
+            collective_id=0, has_side_effects=True, vmem_limit_bytes=48 * 1024 * 1024
         ),
         cost_estimate=pl.CostEstimate(flops=4_000_000_000, bytes_accessed=2_000_000, transcendentals=0),
-    )(activations, grad_out, query_weight, key_weight, value_weight)
+    )(*operands)
 
 
 def solution(mesh):

time: 83 us -> 81 us (0.976)
  local copies, waits for them, and re-layouts: 1.67 us -> 0.71 us
  Pallas kernels: 81.1 us -> 80.2 us
    unnamed x1, local copies, waits for them, and re-layouts: 1.67 us -> 0.71 us
    pallas_call x1, Pallas kernels: 81.1 us -> 80.2 us  [local(): pl.pallas_call(kernel, out_shape=jax.ShapeDtypeStruct((TOK, FEAT), BF16),...]
where the time goes in v3:
time: 81 us; the launch traced here: 80.9 us
  Pallas kernels  80.2 us (99%)
    pallas_call x1, Pallas kernels, local(): pl.pallas_call(kernel, out_shape=jax.ShapeDtypeStruct((TOK, FEAT), BF16),...  80.2 us

profile of v3, /device:TPU:1, one launch (start us, length us, event | category | flops | bytes accessed | tf_op | source)
XLA Modules:
  0.0 80.9 jit_solution(14864209636305873088)
XLA Ops:
  0.0 80.2 %shard_map.55 = bf16[256,512]{1,0:T(8,128)(2,1)S(1)} custom-call(bf16[256,512]{1,0:T(8,128)(2,1)} %a_ref.1, bf16[256,512]{1,0:T(8,128)(2,1)} %go_ref.1, bf16[64,512]{1,0:T(8,128)(2,1)} %wq_ref.1, bf16[64,128]{1,0:T(8,128)(2,1)} %wk_ref.1, bf16[64,128]{1,0:T(8,128)(2,1)} %wv_ref.1), custom_call_target="tpu_custom_call" | custom-call | flops 4000000000 | bytes 2000000 | tf_op jit(solution)/shard_map/pallas_call | solution.py:501
  80.2 0.7 copy.7

commit v4 on v3

--- a/solution.py
+++ b/solution.py
@@ -100,7 +100,7 @@
     for load in loads:
         load.start()
     barrier = pltpu.get_barrier_semaphore()
-    peers = [zr, zl] + [row_peer(d) for d in range(1, ROW)] + [{"y": n_y(d)} for d in range(1, NY)]
+    peers = [zr, zl, yr, yl, xr, xl, sib]
     for peer in peers:
         pl.semaphore_signal(barrier, inc=1, device_id=peer, device_id_type=pl.DeviceIdType.MESH)
 
@@ -171,7 +171,7 @@
         ref = wts.at[y, x, pl.ds(CUT, WROWS - CUT)]
         return same(ref, s_send.at[NY], s_recv.at[NY], sib)
 
-    def core0():
+    def make0():
         slot = lambda d, k, j: 4 + (d * 5 + k) * 4 + j
 
         def has(d, k, j):
@@ -213,34 +213,38 @@
                 for m in (-k, k) if k < 4 else (4,):
                     sib_msg(m, 0).start()
 
-        if CUT < WROWS:
-            lend_msg().start()
-        w_msg(w_ref(0, 0, 0), 0, xr).start()
-        w_msg(w_ref(0, 0, 0), 1, xl).start()
-        y_both(0)
-        z_start()
-        for step in CORE0:
-            if step == "near":
-                x_near()
-            elif step == "far":
-                x_far()
-            elif isinstance(step, int):
-                z_tick(step)
-            else:
-                y_event(*step)
-
-        if CUT < WROWS:
-            lend_msg().wait_send()
-        for i in range(4):
-            dx, half, dev = ((0, None, xr), (0, None, xl), (-1, 0, xr), (1, 1, xl))[i]
-            w_msg(w_ref(0, dx, 0, half), i, dev).wait_send()
-        for k in range(1, 5):
-            for j in range(4):
-                for d in (0, 1):
-                    if has(d, k, j):
-                        y_msg(d, k, j).wait_send()
-
-    def core1():
+        def run():
+            if CUT < WROWS:
+                lend_msg().start()
+            w_msg(w_ref(0, 0, 0), 0, xr).start()
+            w_msg(w_ref(0, 0, 0), 1, xl).start()
+            y_both(0)
+            z_start()
+            for step in CORE0:
+                if step == "near":
+                    x_near()
+                elif step == "far":
+                    x_far()
+                elif isinstance(step, int):
+                    z_tick(step)
+                else:
+                    y_event(*step)
+
+        def drain():
+            if CUT < WROWS:
+                lend_msg().wait_send()
+            for i in range(4):
+                dx, half, dev = ((0, None, xr), (0, None, xl), (-1, 0, xr), (1, 1, xl))[i]
+                w_msg(w_ref(0, dx, 0, half), i, dev).wait_send()
+            for k in range(1, 5):
+                for j in range(4):
+                    for d in (0, 1):
+                        if has(d, k, j):
+                            y_msg(d, k, j).wait_send()
+
+        return run, drain
+
+    def make1():
         def y_msg(d, k):
             dy = (1 - k) if d == 0 else (k - 1)
             half = None if k < 4 else d
@@ -285,26 +289,33 @@
             if k == 4:
                 x_send(4)
 
-        z_start()
-        if CUT < WROWS:
-            lend_msg().wait_recv()
-        y_msg(0, 1).start()
-        y_msg(1, 1).start()
-        x_send(0)
-        for step in CORE1:
-            if isinstance(step, int):
-                z_tick(step)
-            else:
-                (y_event, x_mid, x_end)["yme".index(step[0])](int(step[1:]))
-        for d in (0, 1):
-            for k in range(1, 5):
-                y_msg(d, k).wait_send()
-        for m in range(NY):
-            for msg in x_first(m) + [x_second(m, 0), x_second(m, 1)]:
-                msg.wait_send()
-
-    pl.when(c == 0)(core0)
-    pl.when(c == 1)(core1)
+        def run():
+            z_start()
+            if CUT < WROWS:
+                lend_msg().wait_recv()
+            y_msg(0, 1).start()
+            y_msg(1, 1).start()
+            x_send(0)
+            for step in CORE1:
+                if isinstance(step, int):
+                    z_tick(step)
+                else:
+                    (y_event, x_mid, x_end)["yme".index(step[0])](int(step[1:]))
+
+        def drain():
+            for d in (0, 1):
+                for k in range(1, 5):
+                    y_msg(d, k).wait_send()
+            for m in range(NY):
+                for msg in x_first(m) + [x_second(m, 0), x_second(m, 1)]:
+                    msg.wait_send()
+
+        return run, drain
+
+    run0, drain0 = make0()
+    run1, drain1 = make1()
+    pl.when(c == 0)(run0)
+    pl.when(c == 1)(run1)
 
     def sib_wait(m):
         def wait_for(core):
@@ -343,12 +354,6 @@
     @pl.when(far_y != far_z)
     def _():
         project(far_z)
-
-    for m in range(NY):
-        sib_sent(m)
-    for pair in [(d, k, s) for d in (0, 1) for k in range(1, HALF + 1) for s in range(SUBS)]:
-        if z_has(*pair):
-            z_msg(*pair).wait_send()
 
     qkv[...] = acc[...].astype(BF16)
     head = lambda h: pl.ds(h * HD, HD)
@@ -388,6 +393,8 @@
             dv[...] += tn(s, g_h)
 
     attend(0)
+    pl.when(c == 0)(drain0)
+    pl.when(c == 1)(drain1)
     for d in range(1, ROW):
         e1_wait(d)
     pieces = [in1[i].astype(F32) for i in range(ROW)]
@@ -409,6 +416,11 @@
     in2[y] = jnp.zeros_like(tot)
     attend(1)
     attend(2)
+    for m in range(NY):
+        sib_sent(m)
+    for pair in [(d, k, s) for d in (0, 1) for k in range(1, HALF + 1) for s in range(SUBS)]:
+        if z_has(*pair):
+            z_msg(*pair).wait_send()
     for d in range(1, NY):
         e2_wait(d)
     before = jnp.zeros((HD // ROW, HD), F32)
@@ -436,10 +448,6 @@
     attend(3)
     for d in range(1, ROW):
         e3_wait(d)
-    for d in range(1, ROW):
-        e1(d).wait_send()
-        e2(d).wait_send()
-        e3(d).wait_send()
     prefix = in3[:, 0].reshape(HD, HD)
     suffix = in3[:, 1].reshape(HD, HD)
     for h in range(GROUP):
@@ -473,6 +481,10 @@
             ds = pl.ds(s * PIECE, PIECE)
             tx[d, HALF - 1, ds] = part[0, ds].astype(BF16)
             r_msg(d, HALF, s).start()
+    for d in range(1, ROW):
+        e1(d).wait_send()
+        e2(d).wait_send()
+        e3(d).wait_send()
     for k in range(HALF - 1, 0, -1):
         share(k, 0)
         share(-k, 1)
@@ -480,6 +492,11 @@
             r_step(0, k, L_TURN[i])
             r_step(1, k, R_TURN[i])
     share(0, 0)
+    for d in (0, 1):
+        for k in range(2, HALF + 1):
+            for s in range(PIECES):
+                if r_has(d, k, s):
+                    r_msg(d, k, s).wait_send()
     for i in range(PIECES):
         s = L_TURN[i]
         ds = pl.ds(s * PIECE, PIECE)
@@ -488,10 +505,8 @@
         total = part[0, ds] + rx[0, 0, ds].astype(F32) + rx[1, 0, ds].astype(F32)
         o_ref[ds] = total.astype(BF16)
     for d in (0, 1):
-        for k in range(1, HALF + 1):
-            for s in range(PIECES):
-                if r_has(d, k, s):
-                    r_msg(d, k, s).wait_send()
+        for i in range(PIECES):
+            r_msg(d, 1, i).wait_send()
 
 
 def local(activations, grad_out, query_weight, key_weight, value_weight):

time: 81 us -> 79.5 us (0.981)
  Pallas kernels: 80.2 us -> 78.6 us
    pallas_call x1, Pallas kernels: 80.2 us -> 78.6 us  [local(): pl.pallas_call(kernel, out_shape=jax.ShapeDtypeStruct((TOK, FEAT), BF16),...]
where the time goes in v4:
time: 79.5 us; the launch traced here: 79.4 us
  Pallas kernels  78.6 us (99%)
    pallas_call x1, Pallas kernels, local(): pl.pallas_call(kernel, out_shape=jax.ShapeDtypeStruct((TOK, FEAT), BF16),...  78.6 us

profile of v4, /device:TPU:1, one launch (start us, length us, event | category | flops | bytes accessed | tf_op | source)
XLA Modules:
  0.0 79.4 jit_solution(18370206589410526047)
XLA Ops:
  0.0 78.6 %shard_map.55 = bf16[256,512]{1,0:T(8,128)(2,1)S(1)} custom-call(bf16[256,512]{1,0:T(8,128)(2,1)} %a_ref.1, bf16[256,512]{1,0:T(8,128)(2,1)} %go_ref.1, bf16[64,512]{1,0:T(8,128)(2,1)} %wq_ref.1, bf16[64,128]{1,0:T(8,128)(2,1)} %wk_ref.1, bf16[64,128]{1,0:T(8,128)(2,1)} %wv_ref.1), custom_call_target="tpu_custom_call" | custom-call | flops 4000000000 | bytes 2000000 | tf_op jit(solution)/shard_map/pallas_call | solution.py:516
  78.7 0.7 copy.7

commit v5 on v4

--- a/solution.py
+++ b/solution.py
@@ -97,8 +97,8 @@
         pltpu.make_async_copy(wv_ref, wts.at[y, x, own, pl.ds(640, 128)], i_sem.at[3]),
         pltpu.make_async_copy(go_ref, g_ref, i_sem.at[4]),
     ]
-    for load in loads:
-        load.start()
+    for i in (1, 2, 3, 0, 4):
+        loads[i].start()
     barrier = pltpu.get_barrier_semaphore()
     peers = [zr, zl, yr, yl, xr, xl, sib]
     for peer in peers:
@@ -346,14 +346,15 @@
         def _():
             project(f)
 
+    sib_wait(4)
+
+    @pl.when(far_y != far_z)
+    def _():
+        project(far_y)
+
     z_tick(12)
     z_tick(13)
-    sib_wait(4)
-    project(far_y)
-
-    @pl.when(far_y != far_z)
-    def _():
-        project(far_z)
+    project(far_z)
 
     qkv[...] = acc[...].astype(BF16)
     head = lambda h: pl.ds(h * HD, HD)

time: 79.5 us -> 79.4 us (level)
  no operation moved by 1% of the time
where the time goes in v5:
time: 79.4 us; the launch traced here: 79.3 us
  Pallas kernels  78.6 us (99%)
    pallas_call x1, Pallas kernels, local(): pl.pallas_call(kernel, out_shape=jax.ShapeDtypeStruct((TOK, FEAT), BF16),...  78.6 us

profile of v5, /device:TPU:1, one launch (start us, length us, event | category | flops | bytes accessed | tf_op | source)
XLA Modules:
  0.0 79.3 jit_solution(15305956567199043660)
XLA Ops:
  0.0 78.6 %shard_map.55 = bf16[256,512]{1,0:T(8,128)(2,1)S(1)} custom-call(bf16[256,512]{1,0:T(8,128)(2,1)} %a_ref.1, bf16[256,512]{1,0:T(8,128)(2,1)} %go_ref.1, bf16[64,512]{1,0:T(8,128)(2,1)} %wq_ref.1, bf16[64,128]{1,0:T(8,128)(2,1)} %wk_ref.1, bf16[64,128]{1,0:T(8,128)(2,1)} %wv_ref.1), custom_call_target="tpu_custom_call" | custom-call | flops 4000000000 | bytes 2000000 | tf_op jit(solution)/shard_map/pallas_call | solution.py:517
  78.6 0.7 copy.7

commit v6 on v5

--- a/solution.py
+++ b/solution.py
@@ -89,6 +89,11 @@
     sib = {"core": 1 - c}
     row_peer = lambda d: {"x": n_r(d) // NC, "core": lax.rem(n_r(d), NC)}
 
+    barrier = pltpu.get_barrier_semaphore()
+    peers = [zr, zl, yr, yl, xr, xl, sib]
+    for peer in peers:
+        pl.semaphore_signal(barrier, inc=1, device_id=peer, device_id_type=pl.DeviceIdType.MESH)
+
     own = pl.ds(pl.multiple_of(c * WROWS, WROWS), WROWS)
     loads = [
         pltpu.make_async_copy(a_ref, act.at[z], i_sem.at[0]),
@@ -99,11 +104,6 @@
     ]
     for i in (1, 2, 3, 0, 4):
         loads[i].start()
-    barrier = pltpu.get_barrier_semaphore()
-    peers = [zr, zl, yr, yl, xr, xl, sib]
-    for peer in peers:
-        pl.semaphore_signal(barrier, inc=1, device_id=peer, device_id_type=pl.DeviceIdType.MESH)
-
     pl.semaphore_wait(barrier, len(peers))
     for load in loads[1:4]:
         load.wait()

time: 79.4 us -> 79.5 us (level)
  no operation moved by 1% of the time
where the time goes in v6:
time: 79.5 us; the launch traced here: 79.4 us
  Pallas kernels  78.7 us (99%)
    pallas_call x1, Pallas kernels, local(): pl.pallas_call(kernel, out_shape=jax.ShapeDtypeStruct((TOK, FEAT), BF16),...  78.7 us

profile of v6, /device:TPU:1, one launch (start us, length us, event | category | flops | bytes accessed | tf_op | source)
XLA Modules:
  0.0 79.4 jit_solution(17935294498634493467)
XLA Ops:
  0.0 78.7 %shard_map.55 = bf16[256,512]{1,0:T(8,128)(2,1)S(1)} custom-call(bf16[256,512]{1,0:T(8,128)(2,1)} %a_ref.1, bf16[256,512]{1,0:T(8,128)(2,1)} %go_ref.1, bf16[64,512]{1,0:T(8,128)(2,1)} %wq_ref.1, bf16[64,128]{1,0:T(8,128)(2,1)} %wk_ref.1, bf16[64,128]{1,0:T(8,128)(2,1)} %wv_ref.1), custom_call_target="tpu_custom_call" | custom-call | flops 4000000000 | bytes 2000000 | tf_op jit(solution)/shard_map/pallas_call | solution.py:517
  78.7 0.7 copy.7
